TPU v7x, 256 devices: a whole 4x4x8 slice. The times are simulated.
256 devices in a mesh: row: 8 (over z_hi, core), col: 32 (over x, z_lo, y).
Axes of the slice: x: 4, y: 4, z: 8 (z_hi: 4, z_lo: 2; z = z_hi * 2 + z_lo), core: 2. Of those that a mesh axis runs over, the one named last changes fastest.
Arguments:
- tokens: bfloat16 [2048, 12288], P('col', 'row'), may hold values from -12 to 12
- ln_gain: float32 [12288], P('row'), may hold values from 0.25 to 1.75
- ln_bias: float32 [12288], P('row'), may hold values from -3 to 3
- w_qkv: bfloat16 [3, 12288, 12288], P(None, 'row', 'col'), may hold values from -0.078125 to 0.078125
- bias_qkv: float32 [3, 12288], P(None, 'col'), may hold values from -9 to 9
- mask_qkv: int32 [3, 96, 96], P(None, 'row', 'col'), may hold values from 0 to 1, as said below
- w_out: bfloat16 [12288, 12288], P('col', 'row'), may hold values from -0.078125 to 0.078125
- bias_out: float32 [12288], P('row'), may hold values from -3 to 3
- mask_out: int32 [96, 96], P('col', 'row'), may hold values from 0 to 1, as said below
Outputs:
- mixed: bfloat16 [2048, 12288], P('col', 'row')
Inputs may be any that keep to these rules, and one draw needn't show every extreme that they name: `mask_qkv`: 1 keeps a tile of 128 x 128 weights and 0 prunes it; the kept share differs between the blocks of tiles that the mesh places on different devices. `mask_out`: 1 keeps a tile of 128 x 128 weights and 0 prunes it; the kept share differs between the blocks of tiles that the mesh places on different devices.
All inputs are finite; a program needn't handle non-finite values.
Results may differ from a plain program's by a relative error of at most 0.023.
Values may be sent and summed in bfloat16 or wider, within the bound.
A program may use at most 64 MiB of HBM per device.

v0:
```python
import jax
import jax.numpy as jnp
from jax import lax
from jax.sharding import PartitionSpec as P

TILE = 128
HEAD_DIM = 128


def expand(weights, mask):
    shape = weights.shape
    rows, cols = (mask.shape[-2], mask.shape[-1])
    tiled = weights.reshape(shape[:-2] + (rows, TILE, cols, TILE))
    keep = mask.astype(jnp.bfloat16)[..., :, None, :, None]
    return (tiled * keep).reshape(shape)


def body(tokens, ln_gain, ln_bias, w_qkv, bias_qkv, mask_qkv, w_out, bias_out, mask_out):
    values = tokens.astype(jnp.float32)
    features = values.shape[1] * lax.axis_size("row")
    gathered = lax.all_gather(tokens, "col", axis=0, tiled=True).astype(jnp.float32)
    first, second = lax.psum(
        (jnp.sum(gathered, axis=1), jnp.sum(gathered * gathered, axis=1)), "row"
    )
    mean = first / features
    var = second / features - mean * mean
    scaled = (gathered - mean[:, None]) * lax.rsqrt(var + 1e-05)[:, None]
    normed = (scaled * ln_gain + ln_bias).astype(jnp.bfloat16)
    pruned_qkv = expand(w_qkv, mask_qkv)
    total_rows = normed.shape[0]
    query_rows = total_rows // lax.axis_size("row")
    heads = pruned_qkv.shape[2] // HEAD_DIM
    whole = lax.psum(
        jnp.einsum("td,kdf->tkf", normed, pruned_qkv, preferred_element_type=jnp.float32).astype(
            jnp.bfloat16
        ),
        "row",
    ).astype(jnp.float32)
    qkv = (whole + bias_qkv[None]).astype(jnp.bfloat16)
    query = lax.dynamic_slice_in_dim(qkv[:, 0], lax.axis_index("row") * query_rows, query_rows, 0)
    keys = qkv[:, 1]
    vals = qkv[:, 2]
    query = query.reshape(query_rows, heads, HEAD_DIM)
    keys = keys.reshape(total_rows, heads, HEAD_DIM)
    vals = vals.reshape(total_rows, heads, HEAD_DIM)
    scores = jnp.einsum("qhd,khd->hqk", query, keys, preferred_element_type=jnp.float32)
    scores = scores / jnp.sqrt(jnp.float32(HEAD_DIM))
    query_pos = lax.axis_index("row") * query_rows + jnp.arange(query_rows, dtype=jnp.int32)
    key_pos = jnp.arange(total_rows, dtype=jnp.int32)
    allowed = key_pos[None, :] <= query_pos[:, None]
    scores = jnp.where(allowed[None], scores, -jnp.inf)
    top = jnp.max(scores, axis=2, keepdims=True)
    expo = jnp.exp(scores - top)
    weights = (expo / jnp.sum(expo, axis=2, keepdims=True)).astype(jnp.bfloat16)
    context = jnp.einsum("hqk,khd->qhd", weights, vals, preferred_element_type=jnp.float32)
    context = context.astype(jnp.bfloat16).reshape(query_rows, heads * HEAD_DIM)
    pruned_out = expand(w_out, mask_out)
    partial_out = jnp.dot(
        lax.all_gather(context, "row", axis=0, tiled=True),
        pruned_out,
        preferred_element_type=jnp.float32,
    )
    summed = lax.psum_scatter(
        partial_out.astype(jnp.bfloat16), "col", scatter_dimension=0, tiled=True
    ).astype(jnp.float32)
    return (values + summed + bias_out).astype(jnp.bfloat16)


def solution(mesh):
    placed = (
        P("col", "row"),
        P("row"),
        P("row"),
        P(None, "row", "col"),
        P(None, "col"),
        P(None, "row", "col"),
        P("col", "row"),
        P("row"),
        P("col", "row"),
    )
    return jax.shard_map(
        body, mesh=mesh, in_specs=placed, out_specs=P("col", "row"), check_vma=False
    )
```

profile of v0, /device:TPU:72, one launch (start us, length us, event | category | flops | bytes accessed | tf_op | source)
XLA Modules:
  0.0 588.0 jit_solution(8249895478228121032)
XLA Ops:
  6.5 0.7 all-gather.3.cloned.1.call-update
  7.3 0.7 convert_element_type.45
  8.0 2.9 mul.54
  10.9 7.5 %mul.55 = bf16[3,1536,384]{1,2,0:T(8,128)(2,1)} reshape(bf16[3,12,128,3,128]{2,1,4,3,0:T(8,128)(2,1)} %mul.54) | data formatting | bytes 7077888 | tf_op jit(solution)/shard_map/mul | solution.py:15
  18.4 3.8 copy.13
  22.2 154.4 %all-gather.3.cloned.1.call-done = bf16[2048,1536]{1,0:T(8,128)(2,1)} async-done(((bf16[64,1536]{1,0:T(8,128)(2,1)}), bf16[2048,1536]{1,0:T(8,128)(2,1)}) %all-gather.3.cloned.1.call-update) | async-done | bytes 6291472 | tf_op jit(solution)/shard_map/all_gather | solution.py:21
  176.6 4.6 convert_reduce_fusion
  181.3 24.5 %all-reduce = (f32[2048]{0:T(1024)}, f32[2048]{0:T(1024)}) all-reduce(f32[2048]{0:T(1024)S(1)} %get-tuple-element.6, f32[2048]{0:T(1024)S(1)} %get-tuple-element.5), channel_id=1, replica_groups=mesh['row'=8,'col'=32] {'row'}, use_global_device_ids=true, to_apply=%region_3.0 | all-reduce | flops 4096 | bytes 32768 | tf_op jit(solution)/shard_map/psum | solution.py:22
  205.8 0.7 broadcast_multiply_fusion
  206.5 14.0 %fusion.14 = bf16[2048,3,384]{2,0,1:T(8,128)(2,1)} fusion(bf16[2048,1536]{1,0:T(8,128)(2,1)} %all-gather.3.cloned.1.call-done, f32[1536]{0:T(1024)} %param.11, f32[1536]{0:T(1024)} %param.10, f32[2048]{0:T(1024)S(1)} %get-tuple-element.13, f32[2048]{0:T(1024)S(1)} %get-tuple-element.12, bf16[3,1536,384]{1,2,0:T(8,128)(2,1)S(1)} %copy-done.1, ...), kind=kOutput, calls=%fused_computation.21 | convolution fusion | flops 7276068864 | bytes 18116608 | tf_op jit(solution)/shard_map/td,kdf->tkf/dot_general | solution.py:34
  220.6 0.2 all-gather.5.cloned.1.call-start
  220.8 1.2 iota_compare_fusion
  222.0 124.3 %all-reduce.3.cloned.1.call-done = bf16[2048,3,384]{2,0,1:T(8,128)(2,1)} async-done(((bf16[2048,3,384]{2,0,1:T(8,128)(2,1)}), bf16[2048,3,384]{2,0,1:T(8,128)(2,1)}) %all-reduce.3.cloned.1.call-update) | async-done | bytes 4718608 | tf_op jit(solution)/shard_map/psum | solution.py:33
  346.3 3.2 add_convert_fusion
  349.5 0.5 fusion.28
  350.2 1.7 copy.17
  351.9 0.7 copy.15
  352.6 6.4 %fusion.29 = (f32[3,256]{1,0:T(4,128)S(1)}, f32[3,256,2048]{2,1,0:T(8,128)}) fusion(pred[256,2048]{1,0:T(8,128)(4,1)} %iota_compare_fusion, bf16[256,3,128]{0,2,1:T(8,128)(2,1)S(1)} %bitcast.28, bf16[2048,3,128]{0,2,1:T(8,128)(2,1)} %bitcast.24), kind=kOutput, calls=%fused_computation.40 | convolution fusion | flops 408946688 | bytes 8588288 | tf_op jit(solution)/shard_map/sub | solution.py:53
  359.1 4.8 fusion.23
  364.0 36.7 %all-gather.5.cloned.1.call-done = bf16[2048,384]{0,1:T(8,128)(2,1)} async-done(((bf16[256,384]{0,1:T(8,128)(2,1)}), bf16[2048,384]{0,1:T(8,128)(2,1)}) %all-gather.5.cloned.1.call-update) | async-done | bytes 1572880 | tf_op jit(solution)/shard_map/all_gather | solution.py:59
  400.6 0.3 mul.58
  400.9 7.1 %convolution_convert_fusion = bf16[2048,1536]{1,0:T(8,128)(2,1)} fusion(bf16[2048,384]{0,1:T(8,128)(2,1)} %all-gather.5.cloned.1.call-done, bf16[384,1536]{1,0:T(8,128)(2,1)S(1)} %copy-done.6, bf16[48,8,12,128]{3,2,1,0:T(8,128)(2,1)S(1)} %bitcast.26), kind=kOutput, calls=%fused_computation.10 | convolution fusion | flops 2419654656 | bytes 10223616 | tf_op jit(solution)/shard_map/dot_general | solution.py:58
  408.1 171.7 %reduce-scatter.2.cloned.1.call-done = bf16[64,1536]{1,0:T(8,128)(2,1)} async-done(((bf16[2048,1536]{1,0:T(8,128)(2,1)}), bf16[64,1536]{1,0:T(8,128)(2,1)}) %reduce-scatter.2.cloned.1.call-update) | async-done | bytes 196624 | tf_op jit(solution)/shard_map/reduce_scatter | solution.py:63
  579.8 1.7 add_convert_fusion.1
  (24 shorter events, 0.3 us)
Async XLA Ops:
  6.5 170.1 %all-gather.3.cloned.1.call-start = ((), (), s32[]{:S(2)}) async-start(), calls=%async_computation.1 | async-start | bytes 6488064 | tf_op jit(solution)/shard_map/all_gather | solution.py:21
  7.3 339.0 %all-reduce.3.cloned.1.call-start = ((), (), s32[]{:S(2)}) async-start(), calls=%async_computation.2 | async-start | bytes 9437184 | tf_op jit(solution)/shard_map/psum | solution.py:33
  10.9 7.5 %copy-start = (bf16[3,1536,384]{2,1,0:T(8,128)(2,1)S(1)}, bf16[3,1536,384]{2,1,0:T(8,128)(2,1)}, u32[]{:S(2)}) copy-start(bf16[3,1536,384]{2,1,0:T(8,128)(2,1)} %param.12) | copy-start | bytes 10616836
  22.2 184.3 %copy-start.1 = (bf16[3,1536,384]{1,2,0:T(8,128)(2,1)S(1)}, bf16[3,1536,384]{1,2,0:T(8,128)(2,1)}, u32[]{:S(2)}) copy-start(bf16[3,1536,384]{1,2,0:T(8,128)(2,1)} %copy.13) | copy-start | bytes 10616836
  220.5 125.8 %copy-start.4 = (f32[3,384]{1,0:T(4,128)S(1)}, f32[3,384]{1,0:T(4,128)}, u32[]{:S(2)}) copy-start(f32[3,384]{1,0:T(4,128)} %param.13) | copy-start | bytes 13828
  220.6 180.1 %all-gather.5.cloned.1.call-start = ((), (), s32[]{:S(2)}) async-start(), calls=%async_computation.3 | async-start | bytes 1769472 | tf_op jit(solution)/shard_map/all_gather | solution.py:59
  359.1 4.9 copy-start.5
  359.1 41.8 %copy-start.6 = (bf16[384,1536]{1,0:T(8,128)(2,1)S(1)}, bf16[384,1536]{1,0:T(8,128)(2,1)}, u32[]{:S(2)}) copy-start(bf16[384,1536]{1,0:T(8,128)(2,1)} %param.15) | copy-start | bytes 3538948
  363.9 215.9 %reduce-scatter.2.cloned.1.call-start = ((), (), s32[]{:S(2)}) async-start(), calls=%async_computation.4 | async-start | bytes 6488064 | tf_op jit(solution)/shard_map/reduce_scatter | solution.py:63
  408.1 171.8 %copy-start.2 = (bf16[64,1536]{1,0:T(8,128)(2,1)S(1)}, bf16[64,1536]{1,0:T(8,128)(2,1)}, u32[]{:S(2)}) copy-start(bf16[64,1536]{1,0:T(8,128)(2,1)} %param.9) | copy-start | bytes 589828
  408.1 171.8 %copy-start.3 = (f32[1536]{0:T(1024)S(1)}, f32[1536]{0:T(1024)}, u32[]{:S(2)}) copy-start(f32[1536]{0:T(1024)} %param.16) | copy-start | bytes 18436
Sparse Core Ops, SparseCore 0:
  9.1 167.4 all-gather.2
  220.7 125.5 all-reduce.2
  364.0 36.5 all-gather.4
  408.2 171.5 reduce-scatter.1
where the time goes:
time: 594 us; the launch traced here: 588 us
  waiting for transfers between devices  488 us (82%)
  matrix products  32.4 us (5%)
  blocking collectives  24.5 us (4%)
  local copies, waits for them, and re-layouts  17.6 us (3%)
  between operations  13.2 us (2%)
  other arithmetic  12.1 us (2%)
    reduce_scatter x1, waiting for transfers between devices, body(): lax.psum_scatter(partial_out.astype(jnp.bfloat16), 'col', scatter_dimensi...  172 us
    all_gather x1, waiting for transfers between devices, body(): lax.all_gather(tokens, 'col', axis=0, tiled=True).astype(jnp.float32)  154 us
    psum x1, waiting for transfers between devices, body(): lax.psum(jnp.einsum('td,kdf->tkf', normed, pruned_qkv, preferred_element_...  124 us
    all_gather x1, waiting for transfers between devices, body(): lax.all_gather(context, 'row', axis=0, tiled=True)  36.7 us
    psum x1, blocking collectives, body(): lax.psum((jnp.sum(gathered, axis=1), jnp.sum(gathered * gathered, axis=1)...  24.5 us
    dot_general x1, matrix products, body(): jnp.einsum('td,kdf->tkf', normed, pruned_qkv, preferred_element_type=jnp....  14 us
  transfers between devices with their start and end apart: 4, of which 4 were waited for; matrix products, arithmetic and copies ran while one was open for 3% of the time, Pallas kernels for 0%

commit v1 on v0

v1 whole, which is shorter than its diff:
```python
import functools

import jax
import jax.numpy as jnp
from jax import lax
from jax.experimental import pallas as pl
from jax.experimental.pallas import tpu as pltpu
from jax.sharding import PartitionSpec as P

BF, F32 = jnp.bfloat16, jnp.float32
HD = 128
D = 12288
FEAT = 1536
UNIT = 384
HALF, RING = 2, 4
LAST = None

ORDER_IN = ((0, 0), (1, 0), (0, 1), (0, 3), (1, 1), (1, 3), (0, 2), (1, 2))
ORDER_OUT = ((0, 2), (1, 2), (0, 1), (0, 3), (1, 1), (1, 3), (0, 0), (1, 0))


def kernel(tok, gain, lnb, wqkv, bqkv, mq, wout, bout, mo, out,
           X, W, WO, BH, stat, S, SB, SR, SUP, SDN, UR, HS, HR, Q, KV, C,
           PO, H1, U1, T, H2, U2, Z, ZS, ssem, rsem):
    r, c = lax.axis_index("row"), lax.axis_index("col")
    core, h = r % 2, r // 2
    y, zl, x = c % 4, (c // 4) % 2, c // 8
    sib = (r + 1 - 2 * core, c)
    hup, hdn, hop = ((r + 2) % 8, c), ((r + 6) % 8, c), ((r + 4) % 8, c)
    zpart = (r, c + 4 - 8 * zl)

    def at_x(k):
        return (r, ((x + k) % 4) * 8 + zl * 4 + y)

    def at_y(k):
        return (r, x * 8 + zl * 4 + (y + k) % 4)

    lead, minor = (x, y), (y, x)
    at_lead, at_minor = (at_x, at_y), (at_y, at_x)
    p = (h + 1 + 2 * zl) % 4

    ids = [0]
    pending = []

    def copy(src, dst, to):
        i = ids[0]
        ids[0] += 1
        return pltpu.make_async_remote_copy(
            src_ref=src, dst_ref=dst, send_sem=ssem.at[i], recv_sem=rsem.at[i],
            device_id=to, device_id_type=pl.DeviceIdType.MESH)

    def go(d, cond=None):
        pending.append((d, cond))
        d.start()
        return d

    partners = [sib, hup, hdn, hop, zpart, at_x(1), at_x(3), at_y(1), at_y(3)]
    bar = pltpu.get_barrier_semaphore()
    for d in partners:
        pl.semaphore_signal(bar, inc=1, device_id=d, device_id_type=pl.DeviceIdType.MESH)
    pl.semaphore_wait(bar, len(partners))

    vals = tok[...].astype(F32)
    s1 = jnp.sum(vals, axis=1, keepdims=True)
    s2 = jnp.sum(vals * vals, axis=1, keepdims=True)
    lane = lax.broadcasted_iota(jnp.int32, (64, 128), 1)
    stat[0] = jnp.where(lane < 64, s1, s2)
    d = go(copy(stat.at[0], stat.at[1], sib))
    d.wait_recv()
    stat[2] = stat[0] + stat[1]
    ds = [go(copy(stat.at[2], stat.at[3 + k], to)) for k, to in enumerate((hup, hdn, hop))]
    for d in ds:
        d.wait_recv()
    tot = (stat[2] + stat[3]) + (stat[4] + stat[5])
    mean = tot[:, 0:1] * (1.0 / D)
    var = tot[:, 64:65] * (1.0 / D) - mean * mean
    normed = ((vals - mean) * lax.rsqrt(var + 1e-5) * gain[...] + lnb[...]).astype(BF)
    for hf in range(2):
        X[hf, lead[hf], zl, minor[hf]] = normed[hf * 32:hf * 32 + 32]

    dz, d1 = [], {}
    for hf in range(2):
        ref = X.at[hf, lead[hf], zl, minor[hf]]
        dz.append(go(copy(ref, ref, zpart)))
        for k in (1, 3):
            d1[hf, 0, k] = go(copy(ref, ref, at_minor[hf](k)))

    for i in range(12):
        rows = slice(i * HD, i * HD + HD)
        for a in range(3):
            for k in range(3):
                w = wqkv[k, rows, a * HD:a * HD + HD].astype(F32) * mq[(k * 12 + i) * 3 + a].astype(F32)
                W[rows, a * UNIT + k * HD:a * UNIT + k * HD + HD] = w.astype(BF)
    for a in range(3):
        BH[a] = jnp.broadcast_to(
            jnp.concatenate([bqkv[k:k + 1, a * HD:a * HD + HD] for k in range(3)], axis=1), (8, UNIT))

    for hf in range(2):
        dz[hf].wait_recv()
        ref = X.at[hf, lead[hf], 1 - zl, minor[hf]]
        for k in (1, 3):
            d1[hf, 1, k] = go(copy(ref, ref, at_minor[hf](k)))
    df = {}
    for g in range(2):
        gz = zl if g == 0 else 1 - zl
        step = 1 + 2 * gz
        for hf in range(2):
            for k in (1, 3):
                d1[hf, g, k].wait_recv()
            ref = X.at[hf, lead[hf], gz, (minor[hf] + 4 - step) % 4]
            df[hf, g] = go(copy(ref, ref, at_minor[hf](step)))
    d2 = {}
    for hf in range(2):
        for g in range(2):
            df[hf, g].wait_recv()
    for g in range(2):
        for hf in range(2):
            for k, gg in ((1, g), (3, 1 - g)):
                ref = X.at[hf, lead[hf], gg]
                d2[hf, k, gg] = go(copy(ref, ref, at_lead[hf](k)))

    def forward_lead(hf):
        for k, gg in ((1, 0), (3, 1)):
            d2[hf, k, gg].wait_recv()
            ref = X.at[hf, (lead[hf] + 4 - k) % 4, gg]
            d2[hf, 2, gg] = go(copy(ref, ref, at_lead[hf](k)))

    dsib, dup, ddn, dhup, dhdn, dkv = {}, {}, {}, {}, {}, {}

    def stage_m(t):
        hf, k = ORDER_IN[t]
        l = (lead[hf] + k) % 4
        if k in (1, 3):
            for gg in range(2):
                if (4 - k, gg) not in ((1, 0), (3, 1)):
                    d2[hf, 4 - k, gg].wait_recv()
        elif k == 2:
            for gg in range(2):
                d2[hf, 2, gg].wait_recv()
        rows = jnp.concatenate(
            [X[hf, l, core].reshape(128, FEAT), X[hf, l, 1 - core].reshape(128, FEAT)], axis=0)
        acc = jnp.dot(rows, W[...], preferred_element_type=F32)
        for a in range(3):
            S[t, a] = acc[:128, a * UNIT:a * UNIT + UNIT]
            SB[t, a] = acc[128:, a * UNIT:a * UNIT + UNIT].astype(BF)
        dsib[t] = go(copy(SB.at[t], SR.at[t], sib))

    a_up = jnp.where(p == 1, 1, jnp.where(p == 2, 2, 0))
    a_dn = jnp.where(p == 2, 0, jnp.where(p == 3, 1, 2))

    def stage_e(t):
        dsib[t].wait_recv()
        for a in range(3):
            S[t, a] = S[t, a] + SR[t, a].astype(F32)
        dup[t] = copy(SUP.at[t], UR.at[0, t], hup)
        ddn[t] = copy(SDN.at[t], UR.at[1, t], hdn)
        dhup[t] = copy(HS.at[0, t], HR.at[0, t], hup)
        dhdn[t] = copy(HS.at[1, t], HR.at[1, t], hdn)
        pending.extend([(dup[t], None), (ddn[t], None), (dhup[t], p == 0), (dhdn[t], p == 0)])

        @pl.when(p >= 2)
        def _():
            SUP[t] = S[t, a_up].astype(BF)
            dup[t].start()

        @pl.when((p == 1) | (p == 2))
        def _():
            SDN[t] = S[t, a_dn].astype(BF)
            ddn[t].start()

        @pl.when(p == 0)
        def _():
            HS[0, t] = S[t, 1, 0:64].astype(BF)
            dhup[t].start()
            HS[1, t] = S[t, 1, 64:128].astype(BF)
            dhdn[t].start()

    def stage_f(t):
        @pl.when(p == 0)
        def _():
            dup[t].wait_recv()
            SUP[t] = (S[t, 0] + UR[0, t].astype(F32)).astype(BF)
            dup[t].start()
            ddn[t].wait_recv()
            SDN[t] = (S[t, 2] + UR[1, t].astype(F32)).astype(BF)
            ddn[t].start()

        @pl.when(p == 1)
        def _():
            SUP[t, 64:128] = S[t, 1, 64:128].astype(BF)
            dhup[t].wait_recv()
            SUP[t, 0:64] = (S[t, 1, 0:64] + HR[0, t].astype(F32)).astype(BF)
            dup[t].start()

        @pl.when(p == 3)
        def _():
            SDN[t, 0:64] = S[t, 1, 0:64].astype(BF)
            dhdn[t].wait_recv()
            SDN[t, 64:128] = (S[t, 1, 64:128] + HR[1, t].astype(F32)).astype(BF)
            ddn[t].start()

    def stage_g(t):
        hf, k = ORDER_IN[t]
        l = (lead[hf] + k) % 4
        ref = KV.at[:, l, core, :, 0] if hf == 0 else KV.at[:, :, core, l, 1]
        dkv[t] = copy(ref, ref, sib)
        pending.append((dkv[t], p > 0))

        @pl.when(p > 0)
        def _():
            dup[t].wait_recv()
            ddn[t].wait_recv()
            total = S[t, p - 1] + UR[0, t].astype(F32) + UR[1, t].astype(F32) + BH[p - 1][0:1]
            total = total.astype(BF)
            for m in range(4):
                at = (l, m) if hf == 0 else (m, l)
                part = total[m * 32:m * 32 + 32]
                Q[at[0], at[1], hf] = part[:, 0:HD]
                KV[0, at[0], core, at[1], hf] = part[:, HD:2 * HD]
                KV[1, at[0], core, at[1], hf] = part[:, 2 * HD:]
            dkv[t].start()

    stage_m(0)
    stage_m(1)
    stage_e(0)
    stage_e(1)
    stage_f(0)
    stage_f(1)
    forward_lead(0)
    forward_lead(1)
    for i in range(3):
        for j in range(12):
            blk = (slice(i * HD, i * HD + HD), slice(j * HD, j * HD + HD))
            WO[blk] = (wout[blk].astype(F32) * mo[i * 12 + j].astype(F32)).astype(BF)
    stage_g(0)
    stage_g(1)
    for t in range(2, 8):
        stage_m(t)
        if t >= 3:
            stage_e(t - 1)
        if t >= 4:
            stage_f(t - 2)
        if t >= 5:
            stage_g(t - 3)
    stage_e(7)
    stage_f(6)
    stage_g(5)
    stage_f(7)
    stage_g(6)
    stage_g(7)

    a_own = jnp.where(p > 0, p - 1, 0)

    @pl.when(p > 0)
    def _():
        for t in range(8):
            dkv[t].wait_recv()
        scale = 1.4426950408889634 / (HD ** 0.5)
        for b in range(4):
            n = 512 * (b + 1)
            q = Q[b].reshape(256, HD)
            keys = KV[0, 0:b + 1].reshape(n, HD)
            values = KV[1, 0:b + 1].reshape(n, HD)
            s = lax.dot_general(q, keys, (((1,), (1,)), ((), ())), preferred_element_type=F32)
            qpos = lax.broadcasted_iota(jnp.int32, (256, 512), 0) + core * 256
            kpos = lax.broadcasted_iota(jnp.int32, (256, 512), 1)
            diag = jnp.where(kpos <= qpos, s[:, n - 512:], -jnp.inf)
            s = diag if b == 0 else jnp.concatenate([s[:, :n - 512], diag], axis=1)
            top = jnp.max(s, axis=1, keepdims=True)
            e = jnp.exp2((s - top) * scale)
            inv = 1.0 / jnp.sum(e, axis=1, keepdims=True)
            ctx = jnp.dot((e * inv).astype(BF), values, preferred_element_type=F32).astype(BF)
            ctx = ctx.reshape(4, 2, 32, HD)
            for m in range(4):
                C[0, b, core, a_own, m] = ctx[m, 0]
                C[1, m, core, a_own, b] = ctx[m, 1]

    a_prev = (p + 2) % 4
    a_next = p
    a_opp = (p + 1) % 4
    has_prev, has_next, has_opp = p != 1, p != 3, p != 2
    a_prev, a_next, a_opp = a_prev % 3, a_next % 3, a_opp % 3
    cup, cdn, fup, fdn, cs = {}, {}, {}, {}, {}
    for t in range(8):
        hf, k = ORDER_OUT[t]
        l = (lead[hf] + k) % 4
        ref = C.at[hf, l, core, a_own]
        cup[t], cdn[t] = copy(ref, ref, hup), copy(ref, ref, hdn)
        pending.extend([(cup[t], p > 0), (cdn[t], p > 0)])

        @pl.when(p > 0)
        def _():
            cup[t].start()
            cdn[t].start()

    def stage_a(t):
        hf, k = ORDER_OUT[t]
        l = (lead[hf] + k) % 4
        ref = C.at[hf, l, core, a_prev, 0:2]
        fup[t] = copy(ref, ref, hup)
        ref = C.at[hf, l, core, a_next, 2:4]
        fdn[t] = copy(ref, ref, hdn)
        pending.extend([(fup[t], has_prev), (fdn[t], has_next)])

        @pl.when(has_prev)
        def _():
            cup[t].wait_recv()
            fup[t].start()

        @pl.when(has_next)
        def _():
            cdn[t].wait_recv()
            fdn[t].start()

    def stage_b(t):
        hf, k = ORDER_OUT[t]
        l = (lead[hf] + k) % 4

        @pl.when(has_opp)
        def _():
            fup[t].wait_recv()
            fdn[t].wait_recv()
        ref = C.at[hf, l, core]
        cs[t] = go(copy(ref, ref, sib))

    e1, u1 = {}, {}

    def stage_c(t):
        hf, k = ORDER_OUT[t]
        l = (lead[hf] + k) % 4
        cs[t].wait_recv()
        rows = jnp.concatenate(
            [jnp.concatenate([C[hf, l, g, a].reshape(128, HD) for a in range(3)], axis=1)
             for g in range(2)], axis=0)
        acc = jnp.dot(rows, WO[...], preferred_element_type=F32)
        lo, hi = acc[:128].reshape(4, 32, FEAT), acc[128:].reshape(4, 32, FEAT)
        if k == 2:
            PO[t, 0] = lo.astype(BF)
            e1[hf, 0] = go(copy(PO.at[t, 0], H1.at[hf, 0], at_lead[hf](1)))
            PO[t, 1] = hi.astype(BF)
            e1[hf, 1] = go(copy(PO.at[t, 1], H1.at[hf, 1], at_lead[hf](3)))
        elif k == 1:
            PO[t, 1] = hi.astype(BF)
            u1[hf, 0, 1] = go(copy(PO.at[t, 1], U1.at[hf, 0, 1], at_lead[hf](1)))
            e1[hf, 0].wait_recv()
            PO[t, 0] = (lo + H1[hf, 0].astype(F32)).astype(BF)
            u1[hf, 0, 0] = go(copy(PO.at[t, 0], U1.at[hf, 0, 0], at_lead[hf](1)))
        elif k == 3:
            PO[t, 0] = lo.astype(BF)
            u1[hf, 1, 0] = go(copy(PO.at[t, 0], U1.at[hf, 1, 0], at_lead[hf](3)))
            e1[hf, 1].wait_recv()
            PO[t, 1] = (hi + H1[hf, 1].astype(F32)).astype(BF)
            u1[hf, 1, 1] = go(copy(PO.at[t, 1], U1.at[hf, 1, 1], at_lead[hf](3)))
        else:
            T[hf, 0] = lo
            T[hf, 1] = hi

    for t in range(10):
        if t < 8:
            stage_a(t)
        if 1 <= t < 9:
            stage_b(t - 1)
        if t >= 2:
            stage_c(t - 2)

    e2, u2, ez = {}, {}, {}
    for hf in range(2):
        m, to = minor[hf], at_minor[hf]
        m2, mp, mm = (m + 2) % 4, (m + 1) % 4, (m + 3) % 4
        for dr in range(2):
            for g in range(2):
                u1[hf, dr, g].wait_recv()
        for g in range(2):
            T[hf, g] = T[hf, g] + U1[hf, 0, g].astype(F32) + U1[hf, 1, g].astype(F32)
        ZS[hf, 0, 0] = T[hf, 0, m2].astype(BF)
        ZS[hf, 0, 1] = T[hf, 1, m2].astype(BF)
        e2[hf, 0] = go(copy(ZS.at[hf, 0, 0], H2.at[hf, 0], to(1)))
        e2[hf, 1] = go(copy(ZS.at[hf, 0, 1], H2.at[hf, 1], to(3)))
        ZS[hf, 1, 1] = T[hf, 1, mp].astype(BF)
        ZS[hf, 2, 0] = T[hf, 0, mm].astype(BF)
        u2[hf, 0, 1] = go(copy(ZS.at[hf, 1, 1], U2.at[hf, 0, 1], to(1)))
        u2[hf, 1, 0] = go(copy(ZS.at[hf, 2, 0], U2.at[hf, 1, 0], to(3)))
    for hf in range(2):
        m, to = minor[hf], at_minor[hf]
        mp, mm = (m + 1) % 4, (m + 3) % 4
        e2[hf, 0].wait_recv()
        ZS[hf, 1, 0] = (T[hf, 0, mp] + H2[hf, 0].astype(F32)).astype(BF)
        u2[hf, 0, 0] = go(copy(ZS.at[hf, 1, 0], U2.at[hf, 0, 0], to(1)))
        e2[hf, 1].wait_recv()
        ZS[hf, 2, 1] = (T[hf, 1, mm] + H2[hf, 1].astype(F32)).astype(BF)
        u2[hf, 1, 1] = go(copy(ZS.at[hf, 2, 1], U2.at[hf, 1, 1], to(3)))
    for hf in range(2):
        m = minor[hf]
        for dr in range(2):
            for g in range(2):
                u2[hf, dr, g].wait_recv()
        g = 1 - zl
        ZS[hf, 3, 0] = (T[hf, g, m] + U2[hf, 0, g].astype(F32) + U2[hf, 1, g].astype(F32)).astype(BF)
        ez[hf] = go(copy(ZS.at[hf, 3, 0], Z.at[hf], zpart))
    for hf in range(2):
        m = minor[hf]
        rows = slice(hf * 32, hf * 32 + 32)
        own = T[hf, zl, m] + U2[hf, 0, zl].astype(F32) + U2[hf, 1, zl].astype(F32)
        own = own + tok[rows].astype(F32) + bout[...]
        ez[hf].wait_recv()
        out[rows] = (own + Z[hf].astype(F32)).astype(BF)

    for d, cond in pending:
        if cond is None:
            d.wait_send()
        else:
            pl.when(cond)(d.wait_send)


SCRATCH = [
    pltpu.VMEM((2, 4, 2, 4, 32, FEAT), BF),
    pltpu.VMEM((FEAT, 3 * UNIT), BF),
    pltpu.VMEM((UNIT, FEAT), BF),
    pltpu.VMEM((3, 8, UNIT), F32),
    pltpu.VMEM((6, 64, 128), F32),
    pltpu.VMEM((8, 3, 128, UNIT), F32),
    pltpu.VMEM((8, 3, 128, UNIT), BF),
    pltpu.VMEM((8, 3, 128, UNIT), BF),
    pltpu.VMEM((8, 128, UNIT), BF),
    pltpu.VMEM((8, 128, UNIT), BF),
    pltpu.VMEM((2, 8, 128, UNIT), BF),
    pltpu.VMEM((2, 8, 64, UNIT), BF),
    pltpu.VMEM((2, 8, 64, UNIT), BF),
    pltpu.VMEM((4, 4, 2, 32, HD), BF),
    pltpu.VMEM((2, 4, 2, 4, 2, 32, HD), BF),
    pltpu.VMEM((2, 4, 2, 3, 4, 32, HD), BF),
    pltpu.VMEM((6, 2, 4, 32, FEAT), BF),
    pltpu.VMEM((2, 2, 4, 32, FEAT), BF),
    pltpu.VMEM((2, 2, 2, 4, 32, FEAT), BF),
    pltpu.VMEM((2, 2, 4, 32, FEAT), F32),
    pltpu.VMEM((2, 2, 32, FEAT), BF),
    pltpu.VMEM((2, 2, 2, 32, FEAT), BF),
    pltpu.VMEM((2, 32, FEAT), BF),
    pltpu.VMEM((2, 4, 2, 32, FEAT), BF),
    pltpu.SemaphoreType.DMA((256,)),
    pltpu.SemaphoreType.DMA((256,)),
]


def body(tokens, ln_gain, ln_bias, w_qkv, bias_qkv, mask_qkv, w_out, bias_out, mask_out):
    vm = pl.BlockSpec(memory_space=pltpu.VMEM)
    sm = pl.BlockSpec(memory_space=pltpu.SMEM)
    return pl.pallas_call(
        kernel,
        out_shape=jax.ShapeDtypeStruct((64, FEAT), BF),
        in_specs=[vm, vm, vm, vm, vm, sm, vm, vm, sm],
        out_specs=vm,
        scratch_shapes=SCRATCH,
        compiler_params=pltpu.CompilerParams(
            collective_id=0, has_side_effects=True, vmem_limit_bytes=60 * 1024 * 1024),
    )(tokens, ln_gain.reshape(1, FEAT), ln_bias.reshape(1, FEAT), w_qkv, bias_qkv,
      mask_qkv.reshape(-1), w_out, bias_out.reshape(1, FEAT), mask_out.reshape(-1))


def solution(mesh):
    placed = (
        P("col", "row"),
        P("row"),
        P("row"),
        P(None, "row", "col"),
        P(None, "col"),
        P(None, "row", "col"),
        P("col", "row"),
        P("row"),
        P("col", "row"),
    )
    return jax.shard_map(
        body, mesh=mesh, in_specs=placed, out_specs=P("col", "row"), check_vma=False
    )
```

time: 594 us -> 183 us (0.31)
  the two profiles are of different devices: /device:TPU:72 before, /device:TPU:32 now
where the time goes in v1:
time: 183 us; the launch traced here: 182 us
  Pallas kernels  174 us (95%)
  local copies, waits for them, and re-layouts  8.2 us (4%)
    pallas_call x1, Pallas kernels, body(): pl.pallas_call(kernel, out_shape=jax.ShapeDtypeStruct((64, FEAT), BF), in...  174 us

profile of v1, /device:TPU:32, one launch (start us, length us, event | category | flops | bytes accessed | tf_op | source)
XLA Modules:
  0.0 182.2 jit_solution(17116130022586059751)
XLA Ops:
  0.0 1.3 reshape.19.mo
  1.3 1.3 reshape.15.gain
  2.6 1.3 reshape.16.lnb
  3.9 1.3 reshape.18.bout
  5.2 0.8 copy.11
  6.0 0.6 reshape.17.mq
  6.6 174.0 %shard_map.91 = bf16[64,1536]{1,0:T(8,128)(2,1)} custom-call(bf16[64,1536]{1,0:T(8,128)(2,1)} %tok.1, f32[1,1536]{1,0:T(1,128)} %reshape.15.gain, f32[1,1536]{1,0:T(1,128)} %reshape.16.lnb, bf16[3,1536,384]{2,1,0:T(8,128)(2,1)} %wqkv.1, f32[3,384]{1,0:T(4,128)} %bqkv.1, s32[108]{0:T(128)} %reshape.17.mq, bf16[384,1536]{1,0:T(8,128)(2,1)} %wout.1, ...), custom_call_target="tpu_custom_call" | custom-call | tf_op jit(solution)/shard_map/pallas_call | solution.py:448
  180.6 1.6 copy.13

commit v2 on v1

v2 whole, which is shorter than its diff:
```python
import functools

import jax
import jax.numpy as jnp
from jax import lax
from jax.experimental import pallas as pl
from jax.experimental.pallas import tpu as pltpu
from jax.sharding import PartitionSpec as P

BF, F32 = jnp.bfloat16, jnp.float32
HD = 128
D = 12288
FEAT = 1536
UNIT = 384
HALF, RING = 2, 4

ORDER_IN = tuple((hf, k0, k1, m, 2) for k0, k1 in ((0, 0), (3, 1), (1, 3), (2, 2))
                 for m in (0, 2) for hf in (0, 1))
OFF = [32 * sum(q[4] for q in ORDER_IN[:t]) for t in range(len(ORDER_IN))]
PIECES = len(ORDER_IN)
SCHEDULE = (
    "M0", "M1", "E0", "E1", "M2", "M3", "E2", "E3", "F0", "F1", "P", "F2", "F3", "W", "M4", "M5", "E4", "E5", "M6", "M7", "E6", "E7", "F4", "F5", "M8", "M9", "E8",
    "E9", "F6", "F7", "M10", "M11", "E10", "E11", "F8", "F9", "M12", "M13", "E12", "E13", "F10", "F11", "M14", "M15", "E14", "E15", "F12", "F13",
    "F14", "F15", "G0", "G1", "G2", "G3", "G4", "G5", "G6", "G7", "G8", "G9", "G10", "G11", "G12", "G13", "G14", "G15",
)
SCHEDULE_OUT = (
    "S0", "S1", "B0", "S2", "B1", "S3", "C0", "S4", "C1", "S5", "B2", "C2", "B3", "C3", "S6", "S7",
    "B4", "C4", "B5", "C5", "B6", "B7", "D0", "D1", "D2", "D3", "C6", "C7",
)
ORDER_OUT = ((0, 2), (1, 2), (0, 1), (0, 3), (1, 1), (1, 3), (0, 0), (1, 0))


def kernel(tok, gain, lnb, wqkv_hbm, bqkv, mq, wout_hbm, bout, mo, out,
           wqkv, wout, RZ, X, W, WO, BH, stat, S, SB, SR, SUP, SDN, UR, HS, HR, Q, KV, C,
           PO, H1, U1, T, H2, U2, Z, ZS, ssem, rsem, lsem):
    r, c = lax.axis_index("row"), lax.axis_index("col")
    core, h = r % 2, r // 2
    y, zl, x = c % 4, (c // 4) % 2, c // 8
    sib = (r + 1 - 2 * core, c)
    hup, hdn, hop = ((r + 2) % 8, c), ((r + 6) % 8, c), ((r + 4) % 8, c)
    zpart = (r, c + 4 - 8 * zl)

    def at_x(k):
        return (r, ((x + k) % 4) * 8 + zl * 4 + y)

    def at_y(k):
        return (r, x * 8 + zl * 4 + (y + k) % 4)

    lead, minor = (x, y), (y, x)
    at_lead, at_minor = (at_x, at_y), (at_y, at_x)
    p = (h + 1 + 2 * zl) % 4

    ids = [0]
    pending = []

    def copy(src, dst, to):
        i = ids[0]
        ids[0] += 1
        return pltpu.make_async_remote_copy(
            src_ref=src, dst_ref=dst, send_sem=ssem.at[i], recv_sem=rsem.at[i],
            device_id=to, device_id_type=pl.DeviceIdType.MESH)

    def go(d, cond=None):
        pending.append((d, cond))
        d.start()
        return d

    load_w = pltpu.make_async_copy(wqkv_hbm, wqkv, lsem.at[0])
    load_w.start()
    load_o = pltpu.make_async_copy(wout_hbm, wout, lsem.at[1])
    load_o.start()
    peers = [((r + k) % 8, c) for k in range(1, 8)]
    partners = peers + [zpart, at_x(1), at_x(3), at_y(1), at_y(3)]
    bar = pltpu.get_barrier_semaphore()
    for d in partners:
        pl.semaphore_signal(bar, inc=1, device_id=d, device_id_type=pl.DeviceIdType.MESH)

    vals = tok[...].astype(F32)
    s1 = jnp.sum(vals, axis=1, keepdims=True)
    s2 = jnp.sum(vals * vals, axis=1, keepdims=True)
    lane = lax.broadcasted_iota(jnp.int32, (64, 128), 1)
    line = lax.broadcasted_iota(jnp.int32, (64, 128), 0)
    packed = jnp.where(lane == line, s1, 0.0) + jnp.where(lane == line + 64, s2, 0.0)
    stat[0] = jnp.broadcast_to(jnp.sum(packed, axis=0, keepdims=True), (8, 128))
    pl.semaphore_wait(bar, len(partners))
    ds = [go(copy(stat.at[0], stat.at[k + 1], to)) for k, to in enumerate(peers)]
    raw = go(copy(tok, RZ, zpart))
    tot = stat[0]
    for k, d in enumerate(ds):
        d.wait_recv()
        tot = tot + stat[k + 1]
    stat[8] = tot
    dt = go(copy(stat.at[8], stat.at[9], zpart))

    def normalise(values, sums, gz):
        sums = sums[0:1]
        mean = jnp.sum(jnp.where(lane == line, sums, 0.0), axis=1, keepdims=True) * (1.0 / D)
        square = jnp.sum(jnp.where(lane == line + 64, sums, 0.0), axis=1, keepdims=True) * (1.0 / D)
        var = square - mean * mean
        normed = (values - mean) * lax.rsqrt(var + 1e-5) * gain[...].reshape(1, FEAT) + lnb[...].reshape(1, FEAT)
        normed = normed.astype(BF)
        for hf in range(2):
            X[hf, lead[hf], gz, minor[hf]] = normed[hf * 32:hf * 32 + 32]

    d1 = {}

    def send_minor(g):
        for hf in range(2):
            ref = X.at[hf, lead[hf], zl if g == 0 else 1 - zl, minor[hf]]
            for k in (1, 3):
                d1[hf, g, k] = go(copy(ref, ref, at_minor[hf](k)))

    normalise(vals, tot, zl)
    send_minor(0)
    raw.wait_recv()
    dt.wait_recv()
    normalise(RZ[...].astype(F32), stat[9], 1 - zl)
    send_minor(1)

    load_w.wait()

    def prune_qkv(part):
        for i in part:
            rows = slice(i * HD, i * HD + HD)
            for a in range(3):
                for k in range(3):
                    w = wqkv[k, rows, a * HD:a * HD + HD].astype(F32) * mq[k, a, i].astype(F32)
                    W[rows, a * UNIT + k * HD:a * UNIT + k * HD + HD] = w.astype(BF)

    df = {}
    for g in range(2):
        prune_qkv(range(6 * g, 6 * g + 6))
        gz = zl if g == 0 else 1 - zl
        step = 1 + 2 * gz
        for hf in range(2):
            for k in (1, 3):
                d1[hf, g, k].wait_recv()
            ref = X.at[hf, lead[hf], gz, (minor[hf] + 4 - step) % 4]
            df[hf, g] = go(copy(ref, ref, at_minor[hf](step)))
    for a in range(3):
        BH[a] = jnp.broadcast_to(
            jnp.concatenate([bqkv[k:k + 1, a * HD:a * HD + HD] for k in range(3)], axis=1), (8, UNIT))
    d2 = {}
    for hf in range(2):
        for g in range(2):
            df[hf, g].wait_recv()
    for g in range(2):
        for hf in range(2):
            for k, gg in ((1, g), (3, 1 - g)):
                ref = X.at[hf, lead[hf], gg]
                d2[hf, k, gg] = go(copy(ref, ref, at_lead[hf](k)))

    def forward_lead(hf):
        for k, gg in ((1, 0), (3, 1)):
            d2[hf, k, gg].wait_recv()
            ref = X.at[hf, (lead[hf] + 4 - k) % 4, gg]
            d2[hf, 2, gg] = go(copy(ref, ref, at_lead[hf](k)))

    dsib, dup, ddn, dhup, dhdn, dkv = {}, {}, {}, {}, {}, {}

    waited = {(h_, k_, g_) for h_ in range(2) for k_, g_ in ((1, 0), (3, 1))}

    def span(t):
        n = 32 * ORDER_IN[t][4]
        return n, slice(OFF[t], OFF[t] + n), pl.ds(OFF[t], n), pl.ds(OFF[t] // 2, n // 2)

    def stage_m(t):
        hf, k0, k1, m0, mn = ORDER_IN[t]
        n, at, ds_, _ = span(t)
        for k, gg in ((k0, 0), (k1, 1)):
            if k and (hf, 4 - k, gg) not in waited:
                d2[hf, 4 - k, gg].wait_recv()
                waited.add((hf, 4 - k, gg))
        l = [(lead[hf] + k) % 4 for k in (k0, k1)]
        own, other = jnp.where(core == 0, l[0], l[1]), jnp.where(core == 0, l[1], l[0])
        rows = jnp.concatenate(
            [X[hf, own, core, m0:m0 + mn].reshape(n, FEAT),
             X[hf, other, 1 - core, m0:m0 + mn].reshape(n, FEAT)], axis=0)
        acc = jnp.dot(rows, W[...], preferred_element_type=F32)
        for a in range(3):
            S[a, at] = acc[:n, a * UNIT:a * UNIT + UNIT]
            SB[a, at] = acc[n:, a * UNIT:a * UNIT + UNIT].astype(BF)
        dsib[t] = go(copy(SB.at[:, ds_], SR.at[:, ds_], sib))

    a_up = jnp.where(p == 1, 1, jnp.where(p == 2, 2, 0))
    a_dn = jnp.where(p == 2, 0, jnp.where(p == 3, 1, 2))

    def stage_e(t):
        n, at, ds_, hs_ = span(t)
        mid, low = OFF[t] + n // 2, slice(OFF[t] // 2, OFF[t] // 2 + n // 2)
        dsib[t].wait_recv()
        for a in range(3):
            S[a, at] = S[a, at] + SR[a, at].astype(F32)
        dup[t] = copy(SUP.at[ds_], UR.at[0, ds_], hup)
        ddn[t] = copy(SDN.at[ds_], UR.at[1, ds_], hdn)
        dhup[t] = copy(HS.at[0, hs_], HR.at[0, hs_], hup)
        dhdn[t] = copy(HS.at[1, hs_], HR.at[1, hs_], hdn)
        pending.extend([(dup[t], None), (ddn[t], None), (dhup[t], p == 0), (dhdn[t], p == 0)])

        @pl.when(p >= 2)
        def _():
            SUP[at] = S[a_up, at].astype(BF)
            dup[t].start()

        @pl.when((p == 1) | (p == 2))
        def _():
            SDN[at] = S[a_dn, at].astype(BF)
            ddn[t].start()

        @pl.when(p == 0)
        def _():
            HS[0, low] = S[1, OFF[t]:mid].astype(BF)
            dhup[t].start()
            HS[1, low] = S[1, mid:OFF[t] + n].astype(BF)
            dhdn[t].start()

    def stage_f(t):
        n, at, _, _ = span(t)
        mid, low = OFF[t] + n // 2, slice(OFF[t] // 2, OFF[t] // 2 + n // 2)
        first, second = slice(OFF[t], mid), slice(mid, OFF[t] + n)

        @pl.when(p == 0)
        def _():
            dup[t].wait_recv()
            SUP[at] = (S[0, at] + UR[0, at].astype(F32)).astype(BF)
            dup[t].start()
            ddn[t].wait_recv()
            SDN[at] = (S[2, at] + UR[1, at].astype(F32)).astype(BF)
            ddn[t].start()

        @pl.when(p == 1)
        def _():
            SUP[second] = S[1, second].astype(BF)
            dhup[t].wait_recv()
            SUP[first] = (S[1, first] + HR[0, low].astype(F32)).astype(BF)
            dup[t].start()

        @pl.when(p == 3)
        def _():
            SDN[first] = S[1, first].astype(BF)
            dhdn[t].wait_recv()
            SDN[second] = (S[1, second] + HR[1, low].astype(F32)).astype(BF)
            ddn[t].start()

    def stage_g(t):
        hf, k0, k1, m0, mn = ORDER_IN[t]
        _, at, _, _ = span(t)
        l = (lead[hf] + jnp.where(core == 0, k0, k1)) % 4
        ms = pl.ds(m0, mn)
        ref = KV.at[:, l, core, ms, 0] if hf == 0 else KV.at[:, ms, core, l, 1]
        dkv[t] = copy(ref, ref, sib)
        pending.append((dkv[t], p > 0))

        @pl.when(p > 0)
        def _():
            dup[t].wait_recv()
            ddn[t].wait_recv()
            total = S[p - 1, at] + UR[0, at].astype(F32) + UR[1, at].astype(F32) + BH[p - 1][0:1]
            total = total.astype(BF)
            for m in range(mn):
                where = (l, m0 + m) if hf == 0 else (m0 + m, l)
                part = total[m * 32:m * 32 + 32]
                Q[where[0], where[1], hf] = part[:, 0:HD]
                KV[0, where[0], core, where[1], hf] = part[:, HD:2 * HD]
                KV[1, where[0], core, where[1], hf] = part[:, 2 * HD:]
            dkv[t].start()

    def prune_out():
        load_o.wait()
        for i in range(3):
            for j in range(12):
                blk = (slice(i * HD, i * HD + HD), slice(j * HD, j * HD + HD))
                WO[blk] = (wout[blk].astype(F32) * mo[i, j].astype(F32)).astype(BF)

    def pass_on(t):
        forward_lead(0)
        forward_lead(1)

    stages = dict(M=stage_m, E=stage_e, F=stage_f, G=stage_g, W=pass_on, P=lambda t: prune_out())
    for word in SCHEDULE:
        stages[word[0]](int(word[1:] or 0))

    a_own = jnp.where(p > 0, p - 1, 0)

    @pl.when(p > 0)
    def _():
        for t in range(PIECES):
            dkv[t].wait_recv()
        scale = 1.4426950408889634 / (HD ** 0.5)
        for b in range(4):
            n = 512 * (b + 1)
            q = Q[b].reshape(256, HD)
            keys = KV[0, 0:b + 1].reshape(n, HD)
            values = KV[1, 0:b + 1].reshape(n, HD)
            s = lax.dot_general(q, keys, (((1,), (1,)), ((), ())), preferred_element_type=F32)
            qpos = lax.broadcasted_iota(jnp.int32, (256, 512), 0) + core * 256
            kpos = lax.broadcasted_iota(jnp.int32, (256, 512), 1)
            diag = jnp.where(kpos <= qpos, s[:, n - 512:], -jnp.inf)
            s = diag if b == 0 else jnp.concatenate([s[:, :n - 512], diag], axis=1)
            top = jnp.max(s, axis=1, keepdims=True)
            e = jnp.exp2((s - top) * scale)
            inv = 1.0 / jnp.sum(e, axis=1, keepdims=True)
            ctx = jnp.dot((e * inv).astype(BF), values, preferred_element_type=F32).astype(BF)
            ctx = ctx.reshape(4, 2, 32, HD)
            for m in range(4):
                C[0, b, core, a_own, m] = ctx[m, 0]
                C[1, m, core, a_own, b] = ctx[m, 1]

    dctx, cs = {}, {}

    def send_ctx(t):
        hf, k = ORDER_OUT[t]
        ref = C.at[hf, (lead[hf] + k) % 4, core, a_own]
        dctx[t] = [copy(ref, ref, to) for to in (hup, hdn, hop)]
        pending.extend([(d, p > 0) for d in dctx[t]])

        @pl.when(p > 0)
        def _():
            for d in dctx[t]:
                d.start()

    def stage_b(t):
        hf, k = ORDER_OUT[t]
        for d, cond in zip(dctx[t], (p != 1, p != 3, p != 2)):
            pl.when(cond)(d.wait_recv)
        ref = C.at[hf, (lead[hf] + k) % 4, core]
        cs[t] = go(copy(ref, ref, sib))

    e1, u1 = {}, {}

    def stage_c(t):
        hf, k = ORDER_OUT[t]
        l = (lead[hf] + k) % 4
        cs[t].wait_recv()
        rows = jnp.concatenate(
            [jnp.concatenate([C[hf, l, g, a].reshape(128, HD) for a in range(3)], axis=1)
             for g in range(2)], axis=0)
        acc = jnp.dot(rows, WO[...], preferred_element_type=F32)
        lo, hi = acc[:128].reshape(4, 32, FEAT), acc[128:].reshape(4, 32, FEAT)
        if k == 2:
            PO[t, 0] = lo.astype(BF)
            e1[hf, 0] = go(copy(PO.at[t, 0], H1.at[hf, 0], at_lead[hf](1)))
            PO[t, 1] = hi.astype(BF)
            e1[hf, 1] = go(copy(PO.at[t, 1], H1.at[hf, 1], at_lead[hf](3)))
        elif k == 1:
            PO[t, 1] = hi.astype(BF)
            u1[hf, 0, 1] = go(copy(PO.at[t, 1], U1.at[hf, 0, 1], at_lead[hf](1)))
            PO[t, 0] = lo.astype(BF)
        elif k == 3:
            PO[t, 0] = lo.astype(BF)
            u1[hf, 1, 0] = go(copy(PO.at[t, 0], U1.at[hf, 1, 0], at_lead[hf](3)))
            PO[t, 1] = hi.astype(BF)
        else:
            T[hf, 0] = lo
            T[hf, 1] = hi

    def stage_d(hf, g):
        k = 1 if g == 0 else 3
        t = ORDER_OUT.index((hf, k))
        e1[hf, g].wait_recv()
        PO[t, g] = (PO[t, g].astype(F32) + H1[hf, g].astype(F32)).astype(BF)
        u1[hf, g, g] = go(copy(PO.at[t, g], U1.at[hf, g, g], at_lead[hf](k)))

    stages = dict(S=send_ctx, B=stage_b, C=stage_c, D=lambda i: stage_d(i // 2, i % 2))
    for word in SCHEDULE_OUT:
        stages[word[0]](int(word[1:]))

    e2, u2, ez = {}, {}, {}
    for hf in range(2):
        m, to = minor[hf], at_minor[hf]
        m2, mp, mm = (m + 2) % 4, (m + 1) % 4, (m + 3) % 4
        for dr in range(2):
            for g in range(2):
                u1[hf, dr, g].wait_recv()

        def add(g, mi):
            t_ = T[hf, g, mi] + U1[hf, 0, g, mi].astype(F32) + U1[hf, 1, g, mi].astype(F32)
            T[hf, g, mi] = t_
            return t_.astype(BF)

        ZS[hf, 0, 0] = add(0, m2)
        e2[hf, 0] = go(copy(ZS.at[hf, 0, 0], H2.at[hf, 0], to(1)))
        ZS[hf, 0, 1] = add(1, m2)
        e2[hf, 1] = go(copy(ZS.at[hf, 0, 1], H2.at[hf, 1], to(3)))
        ZS[hf, 1, 1] = add(1, mp)
        u2[hf, 0, 1] = go(copy(ZS.at[hf, 1, 1], U2.at[hf, 0, 1], to(1)))
        ZS[hf, 2, 0] = add(0, mm)
        u2[hf, 1, 0] = go(copy(ZS.at[hf, 2, 0], U2.at[hf, 1, 0], to(3)))
        for g, mi in ((0, mp), (1, mm), (0, m), (1, m)):
            add(g, mi)
    for hf in range(2):
        m, to = minor[hf], at_minor[hf]
        mp, mm = (m + 1) % 4, (m + 3) % 4
        e2[hf, 0].wait_recv()
        ZS[hf, 1, 0] = (T[hf, 0, mp] + H2[hf, 0].astype(F32)).astype(BF)
        u2[hf, 0, 0] = go(copy(ZS.at[hf, 1, 0], U2.at[hf, 0, 0], to(1)))
        e2[hf, 1].wait_recv()
        ZS[hf, 2, 1] = (T[hf, 1, mm] + H2[hf, 1].astype(F32)).astype(BF)
        u2[hf, 1, 1] = go(copy(ZS.at[hf, 2, 1], U2.at[hf, 1, 1], to(3)))
    for hf in range(2):
        m = minor[hf]
        for dr in range(2):
            for g in range(2):
                u2[hf, dr, g].wait_recv()
        g = 1 - zl
        ZS[hf, 3, 0] = (T[hf, g, m] + U2[hf, 0, g].astype(F32) + U2[hf, 1, g].astype(F32)).astype(BF)
        ez[hf] = go(copy(ZS.at[hf, 3, 0], Z.at[hf], zpart))
    for hf in range(2):
        m = minor[hf]
        rows = slice(hf * 32, hf * 32 + 32)
        own = T[hf, zl, m] + U2[hf, 0, zl].astype(F32) + U2[hf, 1, zl].astype(F32)
        own = own + tok[rows].astype(F32) + bout[...].reshape(1, FEAT)
        ez[hf].wait_recv()
        out[rows] = (own + Z[hf].astype(F32)).astype(BF)

    for d, cond in pending:
        if cond is None:
            d.wait_send()
        else:
            pl.when(cond)(d.wait_send)


SCRATCH = [
    pltpu.VMEM((3, FEAT, UNIT), BF),
    pltpu.VMEM((UNIT, FEAT), BF),
    pltpu.VMEM((64, FEAT), BF),
    pltpu.VMEM((2, 4, 2, 4, 32, FEAT), BF),
    pltpu.VMEM((FEAT, 3 * UNIT), BF),
    pltpu.VMEM((UNIT, FEAT), BF),
    pltpu.VMEM((3, 8, UNIT), F32),
    pltpu.VMEM((10, 8, 128), F32),
    pltpu.VMEM((3, 1024, UNIT), F32),
    pltpu.VMEM((3, 1024, UNIT), BF),
    pltpu.VMEM((3, 1024, UNIT), BF),
    pltpu.VMEM((1024, UNIT), BF),
    pltpu.VMEM((1024, UNIT), BF),
    pltpu.VMEM((2, 1024, UNIT), BF),
    pltpu.VMEM((2, 512, UNIT), BF),
    pltpu.VMEM((2, 512, UNIT), BF),
    pltpu.VMEM((4, 4, 2, 32, HD), BF),
    pltpu.VMEM((2, 4, 2, 4, 2, 32, HD), BF),
    pltpu.VMEM((2, 4, 2, 3, 4, 32, HD), BF),
    pltpu.VMEM((6, 2, 4, 32, FEAT), BF),
    pltpu.VMEM((2, 2, 4, 32, FEAT), BF),
    pltpu.VMEM((2, 2, 2, 4, 32, FEAT), BF),
    pltpu.VMEM((2, 2, 4, 32, FEAT), F32),
    pltpu.VMEM((2, 2, 32, FEAT), BF),
    pltpu.VMEM((2, 2, 2, 32, FEAT), BF),
    pltpu.VMEM((2, 32, FEAT), BF),
    pltpu.VMEM((2, 4, 2, 32, FEAT), BF),
    pltpu.SemaphoreType.DMA((256,)),
    pltpu.SemaphoreType.DMA((256,)),
    pltpu.SemaphoreType.DMA((2,)),
]


def body(tokens, ln_gain, ln_bias, w_qkv, bias_qkv, mask_qkv, w_out, bias_out, mask_out):
    vm = pl.BlockSpec(memory_space=pltpu.VMEM)
    hbm = pl.BlockSpec(memory_space=pl.ANY)
    sm = pl.BlockSpec(memory_space=pltpu.SMEM)
    return pl.pallas_call(
        kernel,
        out_shape=jax.ShapeDtypeStruct((64, FEAT), BF),
        in_specs=[vm, vm, vm, hbm, vm, sm, hbm, vm, sm],
        out_specs=vm,
        scratch_shapes=SCRATCH,
        compiler_params=pltpu.CompilerParams(
            collective_id=0, has_side_effects=True, vmem_limit_bytes=60 * 1024 * 1024),
    )(tokens, ln_gain, ln_bias, w_qkv, bias_qkv, jnp.swapaxes(mask_qkv, 1, 2), w_out, bias_out, mask_out)


def solution(mesh):
    placed = (
        P("col", "row"),
        P("row"),
        P("row"),
        P(None, "row", "col"),
        P(None, "col"),
        P(None, "row", "col"),
        P("col", "row"),
        P("row"),
        P("col", "row"),
    )
    return jax.shard_map(
        body, mesh=mesh, in_specs=placed, out_specs=P("col", "row"), check_vma=False
    )
```

time: 183 us -> 149 us (0.81)
  the two profiles are of different devices: /device:TPU:32 before, /device:TPU:72 now
where the time goes in v2:
time: 149 us; the launch traced here: 148 us
  Pallas kernels  146 us (98%)
  local copies, waits for them, and re-layouts  1.62 us (1%)
    pallas_call x1, Pallas kernels, body(): pl.pallas_call(kernel, out_shape=jax.ShapeDtypeStruct((64, FEAT), BF), in...  146 us

profile of v2, /device:TPU:72, one launch (start us, length us, event | category | flops | bytes accessed | tf_op | source)
XLA Modules:
  0.0 147.6 jit_solution(9439315865401269922)
XLA Ops:
  0.0 146.0 %shard_map.91 = bf16[64,1536]{1,0:T(8,128)(2,1)} custom-call(bf16[64,1536]{1,0:T(8,128)(2,1)} %tok.1, f32[1536]{0:T(1024)} %gain.1, f32[1536]{0:T(1024)} %lnb.1, bf16[3,1536,384]{2,1,0:T(8,128)(2,1)} %wqkv_hbm.1, f32[3,384]{1,0:T(4,128)} %bqkv.1, s32[3,3,12]{2,1,0:T(4,128)} %bitcast.1, bf16[384,1536]{1,0:T(8,128)(2,1)} %wout_hbm.1, f32[1536]{0:T(1024)} %bout.1, ...), custom_call_target="tpu_custom_call" | custom-call | tf_op jit(solution)/shard_map/pallas_call | solution.py:461
  146.0 1.6 %copy.11 = bf16[64,1536]{1,0:T(8,128)(2,1)} copy(bf16[64,1536]{1,0:T(8,128)(2,1)} %shard_map.91) | data formatting | bytes 393216

commit v3 on v2

--- a/solution.py
+++ b/solution.py
@@ -14,14 +14,20 @@
 UNIT = 384
 HALF, RING = 2, 4
 
-ORDER_IN = tuple((hf, k0, k1, m, 2) for k0, k1 in ((0, 0), (3, 1), (1, 3), (2, 2))
-                 for m in (0, 2) for hf in (0, 1))
-OFF = [32 * sum(q[4] for q in ORDER_IN[:t]) for t in range(len(ORDER_IN))]
+ORDER_IN = (0, 1, 3, 2) + tuple(
+    (hf, k0, k1, m, 2) for k0, k1 in ((3, 1), (1, 3), (2, 2)) for m in (0, 2) for hf in (0, 1))
+ROWS = 64
+OFF = [ROWS * t for t in range(len(ORDER_IN))]
 PIECES = len(ORDER_IN)
 SCHEDULE = (
-    "M0", "M1", "E0", "E1", "M2", "M3", "E2", "E3", "F0", "F1", "P", "F2", "F3", "W", "M4", "M5", "E4", "E5", "M6", "M7", "E6", "E7", "F4", "F5", "M8", "M9", "E8",
-    "E9", "F6", "F7", "M10", "M11", "E10", "E11", "F8", "F9", "M12", "M13", "E12", "E13", "F10", "F11", "M14", "M15", "E14", "E15", "F12", "F13",
-    "F14", "F15", "G0", "G1", "G2", "G3", "G4", "G5", "G6", "G7", "G8", "G9", "G10", "G11", "G12", "G13", "G14", "G15",
+    "M0", "N0", "E0", "N1", "M1", "M2", "E1", "L0", "E2", "M3", "E3", "F0", "F1", "P0",
+    "K0", "K1", "F2", "H0", "H1", "F3", "W0", "M4", "M5", "E4", "E5", "M6", "M7", "E6",
+    "E7", "F4", "F5", "H2", "H3", "K2", "K3", "M8", "M9", "E8", "E9", "F6", "F7", "H4",
+    "H5", "K4", "K5", "M10", "M11", "E10", "E11", "F8", "F9", "H6", "H7", "K6", "K7", "G0",
+    "G1", "M12", "M13", "E12", "E13", "F10", "F11", "H8", "H9", "K8", "K9", "G2", "G3", "M14",
+    "M15", "E14", "E15", "F12", "F13", "H10", "H11", "K10", "K11", "G4", "G5", "G6", "K12", "G7",
+    "K13", "F14", "H12", "G8", "K14", "F15", "H13", "G9", "K15", "H14", "G10", "H15", "G11", "G12",
+    "G13", "G14", "G15",
 )
 SCHEDULE_OUT = (
     "S0", "S1", "B0", "S2", "B1", "S3", "C0", "S4", "C1", "S5", "B2", "C2", "B3", "C3", "S6", "S7",
@@ -74,6 +80,14 @@
     bar = pltpu.get_barrier_semaphore()
     for d in partners:
         pl.semaphore_signal(bar, inc=1, device_id=d, device_id_type=pl.DeviceIdType.MESH)
+
+    def prune_qkv(part):
+        for i in part:
+            rows = slice(i * HD, i * HD + HD)
+            for a in range(3):
+                for k in range(3):
+                    w = wqkv[k, rows, a * HD:a * HD + HD].astype(F32) * mq[k, a, i].astype(F32)
+                    W[rows, a * UNIT + k * HD:a * UNIT + k * HD + HD] = w.astype(BF)
 
     vals = tok[...].astype(F32)
     s1 = jnp.sum(vals, axis=1, keepdims=True)
@@ -85,6 +99,11 @@
     pl.semaphore_wait(bar, len(partners))
     ds = [go(copy(stat.at[0], stat.at[k + 1], to)) for k, to in enumerate(peers)]
     raw = go(copy(tok, RZ, zpart))
+    load_w.wait()
+    prune_qkv(range(0, 6))
+    for a in range(3):
+        BH[a] = jnp.broadcast_to(
+            jnp.concatenate([bqkv[k:k + 1, a * HD:a * HD + HD] for k in range(3)], axis=1), (8, UNIT))
     tot = stat[0]
     for k, d in enumerate(ds):
         d.wait_recv()
@@ -112,24 +131,15 @@
 
     normalise(vals, tot, zl)
     send_minor(0)
+    prune_qkv(range(6, 12))
     raw.wait_recv()
     dt.wait_recv()
     normalise(RZ[...].astype(F32), stat[9], 1 - zl)
     send_minor(1)
 
-    load_w.wait()
-
-    def prune_qkv(part):
-        for i in part:
-            rows = slice(i * HD, i * HD + HD)
-            for a in range(3):
-                for k in range(3):
-                    w = wqkv[k, rows, a * HD:a * HD + HD].astype(F32) * mq[k, a, i].astype(F32)
-                    W[rows, a * UNIT + k * HD:a * UNIT + k * HD + HD] = w.astype(BF)
-
-    df = {}
-    for g in range(2):
-        prune_qkv(range(6 * g, 6 * g + 6))
+    df, d2 = {}, {}
+
+    def pass_minor(g):
         gz = zl if g == 0 else 1 - zl
         step = 1 + 2 * gz
         for hf in range(2):
@@ -137,18 +147,16 @@
                 d1[hf, g, k].wait_recv()
             ref = X.at[hf, lead[hf], gz, (minor[hf] + 4 - step) % 4]
             df[hf, g] = go(copy(ref, ref, at_minor[hf](step)))
-    for a in range(3):
-        BH[a] = jnp.broadcast_to(
-            jnp.concatenate([bqkv[k:k + 1, a * HD:a * HD + HD] for k in range(3)], axis=1), (8, UNIT))
-    d2 = {}
-    for hf in range(2):
+
+    def send_lead(_):
+        for hf in range(2):
+            for g in range(2):
+                df[hf, g].wait_recv()
         for g in range(2):
-            df[hf, g].wait_recv()
-    for g in range(2):
-        for hf in range(2):
-            for k, gg in ((1, g), (3, 1 - g)):
-                ref = X.at[hf, lead[hf], gg]
-                d2[hf, k, gg] = go(copy(ref, ref, at_lead[hf](k)))
+            for hf in range(2):
+                for k, gg in ((1, g), (3, 1 - g)):
+                    ref = X.at[hf, lead[hf], gg]
+                    d2[hf, k, gg] = go(copy(ref, ref, at_lead[hf](k)))
 
     def forward_lead(hf):
         for k, gg in ((1, 0), (3, 1)):
@@ -161,29 +169,31 @@
     waited = {(h_, k_, g_) for h_ in range(2) for k_, g_ in ((1, 0), (3, 1))}
 
     def span(t):
-        n = 32 * ORDER_IN[t][4]
+        n = ROWS
         return n, slice(OFF[t], OFF[t] + n), pl.ds(OFF[t], n), pl.ds(OFF[t] // 2, n // 2)
 
     def stage_m(t):
-        hf, k0, k1, m0, mn = ORDER_IN[t]
         n, at, ds_, _ = span(t)
-        for k, gg in ((k0, 0), (k1, 1)):
-            if k and (hf, 4 - k, gg) not in waited:
-                d2[hf, 4 - k, gg].wait_recv()
-                waited.add((hf, 4 - k, gg))
-        l = [(lead[hf] + k) % 4 for k in (k0, k1)]
-        own, other = jnp.where(core == 0, l[0], l[1]), jnp.where(core == 0, l[1], l[0])
-        rows = jnp.concatenate(
-            [X[hf, own, core, m0:m0 + mn].reshape(n, FEAT),
-             X[hf, other, 1 - core, m0:m0 + mn].reshape(n, FEAT)], axis=0)
+        if t < 4:
+            k = ORDER_IN[t]
+            rows = jnp.concatenate(
+                [X[hf, lead[hf], z, (minor[hf] + k) % 4] for z in (core, 1 - core) for hf in range(2)], axis=0)
+        else:
+            hf, k0, k1, m0, mn = ORDER_IN[t]
+            for k, gg in ((k0, 0), (k1, 1)):
+                if (hf, 4 - k, gg) not in waited:
+                    d2[hf, 4 - k, gg].wait_recv()
+                    waited.add((hf, 4 - k, gg))
+            l = [(lead[hf] + k) % 4 for k in (k0, k1)]
+            own, other = jnp.where(core == 0, l[0], l[1]), jnp.where(core == 0, l[1], l[0])
+            rows = jnp.concatenate(
+                [X[hf, own, core, m0:m0 + mn].reshape(n, FEAT),
+                 X[hf, other, 1 - core, m0:m0 + mn].reshape(n, FEAT)], axis=0)
         acc = jnp.dot(rows, W[...], preferred_element_type=F32)
         for a in range(3):
             S[a, at] = acc[:n, a * UNIT:a * UNIT + UNIT]
             SB[a, at] = acc[n:, a * UNIT:a * UNIT + UNIT].astype(BF)
         dsib[t] = go(copy(SB.at[:, ds_], SR.at[:, ds_], sib))
-
-    a_up = jnp.where(p == 1, 1, jnp.where(p == 2, 2, 0))
-    a_dn = jnp.where(p == 2, 0, jnp.where(p == 3, 1, 2))
 
     def stage_e(t):
         n, at, ds_, hs_ = span(t)
@@ -197,14 +207,14 @@
         dhdn[t] = copy(HS.at[1, hs_], HR.at[1, hs_], hdn)
         pending.extend([(dup[t], None), (ddn[t], None), (dhup[t], p == 0), (dhdn[t], p == 0)])
 
-        @pl.when(p >= 2)
-        def _():
-            SUP[at] = S[a_up, at].astype(BF)
+        @pl.when(p == 3)
+        def _():
+            SUP[at] = S[0, at].astype(BF)
             dup[t].start()
 
-        @pl.when((p == 1) | (p == 2))
-        def _():
-            SDN[at] = S[a_dn, at].astype(BF)
+        @pl.when(p == 1)
+        def _():
+            SDN[at] = S[2, at].astype(BF)
             ddn[t].start()
 
         @pl.when(p == 0)
@@ -214,10 +224,18 @@
             HS[1, low] = S[1, mid:OFF[t] + n].astype(BF)
             dhdn[t].start()
 
+    def stage_k(t):
+        _, at, _, _ = span(t)
+
+        @pl.when(p == 2)
+        def _():
+            SUP[at] = S[2, at].astype(BF)
+            dup[t].start()
+            SDN[at] = S[0, at].astype(BF)
+            ddn[t].start()
+
     def stage_f(t):
-        n, at, _, _ = span(t)
-        mid, low = OFF[t] + n // 2, slice(OFF[t] // 2, OFF[t] // 2 + n // 2)
-        first, second = slice(OFF[t], mid), slice(mid, OFF[t] + n)
+        _, at, _, _ = span(t)
 
         @pl.when(p == 0)
         def _():
@@ -228,6 +246,11 @@
             SDN[at] = (S[2, at] + UR[1, at].astype(F32)).astype(BF)
             ddn[t].start()
 
+    def stage_h(t):
+        n, at, _, _ = span(t)
+        mid, low = OFF[t] + n // 2, slice(OFF[t] // 2, OFF[t] // 2 + n // 2)
+        first, second = slice(OFF[t], mid), slice(mid, OFF[t] + n)
+
         @pl.when(p == 1)
         def _():
             SUP[second] = S[1, second].astype(BF)
@@ -243,13 +266,19 @@
             ddn[t].start()
 
     def stage_g(t):
-        hf, k0, k1, m0, mn = ORDER_IN[t]
         _, at, _, _ = span(t)
-        l = (lead[hf] + jnp.where(core == 0, k0, k1)) % 4
-        ms = pl.ds(m0, mn)
-        ref = KV.at[:, l, core, ms, 0] if hf == 0 else KV.at[:, ms, core, l, 1]
-        dkv[t] = copy(ref, ref, sib)
-        pending.append((dkv[t], p > 0))
+        if t < 4:
+            k = ORDER_IN[t]
+            blocks = ((x, (y + k) % 4, 0), ((x + k) % 4, y, 1))
+            refs = [KV.at[:, bx, core, by, hf] for bx, by, hf in blocks]
+        else:
+            hf, k0, k1, m0, mn = ORDER_IN[t]
+            l = (lead[hf] + jnp.where(core == 0, k0, k1)) % 4
+            ms = pl.ds(m0, mn)
+            refs = [KV.at[:, l, core, ms, 0] if hf == 0 else KV.at[:, ms, core, l, 1]]
+            blocks = [(l, m0 + m, 0) if hf == 0 else (m0 + m, l, 1) for m in range(mn)]
+        dkv[t] = [copy(ref, ref, sib) for ref in refs]
+        pending.extend([(d, p > 0) for d in dkv[t]])
 
         @pl.when(p > 0)
         def _():
@@ -257,13 +286,13 @@
             ddn[t].wait_recv()
             total = S[p - 1, at] + UR[0, at].astype(F32) + UR[1, at].astype(F32) + BH[p - 1][0:1]
             total = total.astype(BF)
-            for m in range(mn):
-                where = (l, m0 + m) if hf == 0 else (m0 + m, l)
+            for m, (bx, by, hf) in enumerate(blocks):
                 part = total[m * 32:m * 32 + 32]
-                Q[where[0], where[1], hf] = part[:, 0:HD]
-                KV[0, where[0], core, where[1], hf] = part[:, HD:2 * HD]
-                KV[1, where[0], core, where[1], hf] = part[:, 2 * HD:]
-            dkv[t].start()
+                Q[bx, by, hf] = part[:, 0:HD]
+                KV[0, bx, core, by, hf] = part[:, HD:2 * HD]
+                KV[1, bx, core, by, hf] = part[:, 2 * HD:]
+            for d in dkv[t]:
+                d.start()
 
     def prune_out():
         load_o.wait()
@@ -276,16 +305,17 @@
         forward_lead(0)
         forward_lead(1)
 
-    stages = dict(M=stage_m, E=stage_e, F=stage_f, G=stage_g, W=pass_on, P=lambda t: prune_out())
+    stages = dict(N=pass_minor, L=send_lead, M=stage_m, E=stage_e, F=stage_f, H=stage_h, K=stage_k, G=stage_g, W=pass_on, P=lambda t: prune_out())
     for word in SCHEDULE:
-        stages[word[0]](int(word[1:] or 0))
+        stages[word[0]](int(word[1:]))
 
     a_own = jnp.where(p > 0, p - 1, 0)
 
     @pl.when(p > 0)
     def _():
         for t in range(PIECES):
-            dkv[t].wait_recv()
+            for d in dkv[t]:
+                d.wait_recv()
         scale = 1.4426950408889634 / (HD ** 0.5)
         for b in range(4):
             n = 512 * (b + 1)
@@ -358,36 +388,40 @@
         k = 1 if g == 0 else 3
         t = ORDER_OUT.index((hf, k))
         e1[hf, g].wait_recv()
-        PO[t, g] = (PO[t, g].astype(F32) + H1[hf, g].astype(F32)).astype(BF)
-        u1[hf, g, g] = go(copy(PO.at[t, g], U1.at[hf, g, g], at_lead[hf](k)))
+        for step in (2, 1, 3, 0):
+            mi = (minor[hf] + step) % 4
+            PO[t, g, mi] = (PO[t, g, mi].astype(F32) + H1[hf, g, mi].astype(F32)).astype(BF)
+            u1[hf, g, g, step] = go(copy(PO.at[t, g, mi], U1.at[hf, g, g, mi], at_lead[hf](k)))
 
     stages = dict(S=send_ctx, B=stage_b, C=stage_c, D=lambda i: stage_d(i // 2, i % 2))
     for word in SCHEDULE_OUT:
         stages[word[0]](int(word[1:]))
 
     e2, u2, ez = {}, {}, {}
+
+    def add(hf, g, step):
+        mi = (minor[hf] + step) % 4
+        u1[hf, g, g, step].wait_recv()
+        t_ = T[hf, g, mi] + U1[hf, 0, g, mi].astype(F32) + U1[hf, 1, g, mi].astype(F32)
+        T[hf, g, mi] = t_
+        return t_.astype(BF)
+
     for hf in range(2):
-        m, to = minor[hf], at_minor[hf]
-        m2, mp, mm = (m + 2) % 4, (m + 1) % 4, (m + 3) % 4
-        for dr in range(2):
-            for g in range(2):
-                u1[hf, dr, g].wait_recv()
-
-        def add(g, mi):
-            t_ = T[hf, g, mi] + U1[hf, 0, g, mi].astype(F32) + U1[hf, 1, g, mi].astype(F32)
-            T[hf, g, mi] = t_
-            return t_.astype(BF)
-
-        ZS[hf, 0, 0] = add(0, m2)
-        e2[hf, 0] = go(copy(ZS.at[hf, 0, 0], H2.at[hf, 0], to(1)))
-        ZS[hf, 0, 1] = add(1, m2)
-        e2[hf, 1] = go(copy(ZS.at[hf, 0, 1], H2.at[hf, 1], to(3)))
-        ZS[hf, 1, 1] = add(1, mp)
+        to = at_minor[hf]
+        u1[hf, 0, 1].wait_recv()
+        u1[hf, 1, 0].wait_recv()
+        for g in range(2):
+            ZS[hf, 0, g] = add(hf, g, 2)
+            e2[hf, g] = go(copy(ZS.at[hf, 0, g], H2.at[hf, g], to(1 + 2 * g)))
+    for hf in range(2):
+        to = at_minor[hf]
+        ZS[hf, 1, 1] = add(hf, 1, 1)
         u2[hf, 0, 1] = go(copy(ZS.at[hf, 1, 1], U2.at[hf, 0, 1], to(1)))
-        ZS[hf, 2, 0] = add(0, mm)
+        ZS[hf, 2, 0] = add(hf, 0, 3)
         u2[hf, 1, 0] = go(copy(ZS.at[hf, 2, 0], U2.at[hf, 1, 0], to(3)))
-        for g, mi in ((0, mp), (1, mm), (0, m), (1, m)):
-            add(g, mi)
+    for hf in range(2):
+        for g, step in ((0, 1), (1, 3), (0, 0), (1, 0)):
+            add(hf, g, step)
     for hf in range(2):
         m, to = minor[hf], at_minor[hf]
         mp, mm = (m + 1) % 4, (m + 3) % 4

time: 149 us -> 144 us (0.966)
  Pallas kernels: 146 us -> 142 us
    pallas_call x1, Pallas kernels: 146 us -> 142 us  [body(): pl.pallas_call(kernel, out_shape=jax.ShapeDtypeStruct((64, FEAT), BF), in...]
where the time goes in v3:
time: 144 us
  Pallas kernels  142 us (99%)
  local copies, waits for them, and re-layouts  1.62 us (1%)
    pallas_call x1, Pallas kernels, body(): pl.pallas_call(kernel, out_shape=jax.ShapeDtypeStruct((64, FEAT), BF), in...  142 us

profile of v3, /device:TPU:72, one launch (start us, length us, event | category | flops | bytes accessed | tf_op | source)
XLA Modules:
  0.0 143.9 jit_solution(7130871214533582099)
XLA Ops:
  0.0 142.3 %shard_map.91 = bf16[64,1536]{1,0:T(8,128)(2,1)} custom-call(bf16[64,1536]{1,0:T(8,128)(2,1)} %tok.1, f32[1536]{0:T(1024)} %gain.1, f32[1536]{0:T(1024)} %lnb.1, bf16[3,1536,384]{2,1,0:T(8,128)(2,1)} %wqkv_hbm.1, f32[3,384]{1,0:T(4,128)} %bqkv.1, s32[3,3,12]{2,1,0:T(4,128)} %bitcast.1, bf16[384,1536]{1,0:T(8,128)(2,1)} %wout_hbm.1, f32[1536]{0:T(1024)} %bout.1, ...), custom_call_target="tpu_custom_call" | custom-call | tf_op jit(solution)/shard_map/pallas_call | solution.py:495
  142.3 1.6 %copy.11 = bf16[64,1536]{1,0:T(8,128)(2,1)} copy(bf16[64,1536]{1,0:T(8,128)(2,1)} %shard_map.91) | data formatting | bytes 393216

commit v4 on v3

--- a/solution.py
+++ b/solution.py
@@ -330,7 +330,7 @@
             top = jnp.max(s, axis=1, keepdims=True)
             e = jnp.exp2((s - top) * scale)
             inv = 1.0 / jnp.sum(e, axis=1, keepdims=True)
-            ctx = jnp.dot((e * inv).astype(BF), values, preferred_element_type=F32).astype(BF)
+            ctx = (jnp.dot(e.astype(BF), values, preferred_element_type=F32) * inv).astype(BF)
             ctx = ctx.reshape(4, 2, 32, HD)
             for m in range(4):
                 C[0, b, core, a_own, m] = ctx[m, 0]
@@ -362,27 +362,20 @@
         hf, k = ORDER_OUT[t]
         l = (lead[hf] + k) % 4
         cs[t].wait_recv()
-        rows = jnp.concatenate(
-            [jnp.concatenate([C[hf, l, g, a].reshape(128, HD) for a in range(3)], axis=1)
-             for g in range(2)], axis=0)
-        acc = jnp.dot(rows, WO[...], preferred_element_type=F32)
-        lo, hi = acc[:128].reshape(4, 32, FEAT), acc[128:].reshape(4, 32, FEAT)
-        if k == 2:
-            PO[t, 0] = lo.astype(BF)
-            e1[hf, 0] = go(copy(PO.at[t, 0], H1.at[hf, 0], at_lead[hf](1)))
-            PO[t, 1] = hi.astype(BF)
-            e1[hf, 1] = go(copy(PO.at[t, 1], H1.at[hf, 1], at_lead[hf](3)))
-        elif k == 1:
-            PO[t, 1] = hi.astype(BF)
-            u1[hf, 0, 1] = go(copy(PO.at[t, 1], U1.at[hf, 0, 1], at_lead[hf](1)))
-            PO[t, 0] = lo.astype(BF)
-        elif k == 3:
-            PO[t, 0] = lo.astype(BF)
-            u1[hf, 1, 0] = go(copy(PO.at[t, 0], U1.at[hf, 1, 0], at_lead[hf](3)))
-            PO[t, 1] = hi.astype(BF)
-        else:
-            T[hf, 0] = lo
-            T[hf, 1] = hi
+
+        def project(g):
+            rows = jnp.concatenate([C[hf, l, g, a].reshape(128, HD) for a in range(3)], axis=1)
+            return jnp.dot(rows, WO[...], preferred_element_type=F32).reshape(4, 32, FEAT)
+
+        for g in ((1, 0) if k == 1 else (0, 1)):
+            if k == 0:
+                T[hf, g] = project(g)
+                continue
+            PO[t, g] = project(g).astype(BF)
+            if k == 2:
+                e1[hf, g] = go(copy(PO.at[t, g], H1.at[hf, g], at_lead[hf](1 + 2 * g)))
+            elif (k, g) in ((1, 1), (3, 0)):
+                u1[hf, 1 - g, g] = go(copy(PO.at[t, g], U1.at[hf, 1 - g, g], at_lead[hf](k)))
 
     def stage_d(hf, g):
         k = 1 if g == 0 else 3

time: 144 us -> 143 us (level)
  no operation moved by 1% of the time
where the time goes in v4:
time: 143 us
  Pallas kernels  141 us (99%)
  local copies, waits for them, and re-layouts  1.62 us (1%)
    pallas_call x1, Pallas kernels, body(): pl.pallas_call(kernel, out_shape=jax.ShapeDtypeStruct((64, FEAT), BF), in...  141 us

profile of v4, /device:TPU:72, one launch (start us, length us, event | category | flops | bytes accessed | tf_op | source)
XLA Modules:
  0.0 142.9 jit_solution(12665870424299545222)
XLA Ops:
  0.0 141.3 %shard_map.91 = bf16[64,1536]{1,0:T(8,128)(2,1)} custom-call(bf16[64,1536]{1,0:T(8,128)(2,1)} %tok.1, f32[1536]{0:T(1024)} %gain.1, f32[1536]{0:T(1024)} %lnb.1, bf16[3,1536,384]{2,1,0:T(8,128)(2,1)} %wqkv_hbm.1, f32[3,384]{1,0:T(4,128)} %bqkv.1, s32[3,3,12]{2,1,0:T(4,128)} %bitcast.1, bf16[384,1536]{1,0:T(8,128)(2,1)} %wout_hbm.1, f32[1536]{0:T(1024)} %bout.1, ...), custom_call_target="tpu_custom_call" | custom-call | tf_op jit(solution)/shard_map/pallas_call | solution.py:488
  141.3 1.6 %copy.11 = bf16[64,1536]{1,0:T(8,128)(2,1)} copy(bf16[64,1536]{1,0:T(8,128)(2,1)} %shard_map.91) | data formatting | bytes 393216
